TPU v7x, 32 devices: a whole 2x2x4 slice. The times are simulated.
32 devices in a mesh: parts: 2 (over x), space: 16 (over z, y, core).
Axes of the slice: x: 2, y: 2, z: 4, core: 2. Of those that a mesh axis runs over, the one named last changes fastest.
Arguments:
- coefficients: bfloat16 [64, 4096], P('parts'), parts along dimension 0, may hold values from -6 to 6
- kl_modes: bfloat16 [8192, 2048], P('parts', 'space'), parts along dimension 0, may hold values from -0.09375 to 0.09375
- green: bfloat16 [4096, 256, 128], P(('parts', 'space')), parts along dimension 0, may hold values from -0.1875 to 0.1875
- sub_index: int32 [4096], P('parts'), parts along dimension 0, may hold values from 0 to 2047, each once
- kernel: float32 [33, 33], replicated, may hold values from 0.2 to 5
- wet_mask: int32 [512, 128], P(('parts', 'space')), parts along dimension 0, may hold values 0 or 1
Outputs:
- surface: float32 [64, 256, 128], P('parts', 'space'), parts along dimension 0
There are 2 independent parts, one for each index of `parts`. A program takes and returns all parts, laid end to end along the dimension named above; an argument that names none is the same for every part. Nothing has to cross between parts.
Inputs may be any that keep to these rules, and one draw needn't show every extreme that they name: `sub_index`: each subfault appears once.
All inputs are finite; a program needn't handle non-finite values. No bound on the sum of `wet_mask` on one device may be relied on, other than what follows from the above.
Results may differ from a plain program's by a relative error of at most 0.005.
Values may be sent and summed in bfloat16 or wider, within the bound.
A program may use at most 128 MiB of HBM per device.

v0:
```python
import jax
import jax.numpy as jnp
from jax import lax
from jax.sharding import PartitionSpec as P


def with_halo(block, sides, width):
    for axis, dim in sides:
        count = lax.axis_size(axis)
        forward = [(i, i + 1) for i in range(count - 1)]
        backward = [(target, source) for source, target in forward]
        low = lax.ppermute(
            lax.slice_in_dim(block, block.shape[dim] - width, None, axis=dim), axis, forward
        )
        high = lax.ppermute(lax.slice_in_dim(block, 0, width, axis=dim), axis, backward)
        block = jnp.concatenate([low, block, high], axis=dim)
    return block


def make_bands(weights, width):
    half = weights.shape[1] // 2
    source = lax.broadcasted_iota(jnp.int32, (width, width), 0)
    target = lax.broadcasted_iota(jnp.int32, (width, width), 1)
    offset = source - target + half
    inside = (offset >= 0) & (offset <= 2 * half)
    picked = jnp.take(weights, jnp.clip(offset, 0, 2 * half), axis=1)
    return jnp.where(inside[None], picked, jnp.zeros_like(picked))


def on_device(coefficients, kl_modes, green, sub_index, kernel, wet_mask):
    realizations = coefficients.shape[0]
    group = green.shape[0]
    width = green.shape[2]
    rows_here = wet_mask.shape[0]
    field = jnp.dot(coefficients, kl_modes, preferred_element_type=jnp.float32)
    slip = jnp.exp(0.5 * field).astype(jnp.bfloat16)
    slip_all = lax.all_gather(slip, "space", axis=1, tiled=True)
    row_ids = lax.dynamic_slice_in_dim(sub_index, lax.axis_index("space") * group, group)
    slip_rows = jnp.take(slip_all, row_ids, axis=1)
    partial_value = jnp.dot(slip_rows, green.reshape(group, -1), preferred_element_type=jnp.float32)
    partial_value = partial_value.reshape(realizations, green.shape[1], width)
    uplift = lax.psum_scatter(partial_value, "space", scatter_dimension=1, tiled=True)
    seafloor = uplift.astype(jnp.bfloat16)
    taps = kernel.shape[0]
    half = taps // 2
    weights = (kernel / jnp.sum(kernel)).astype(jnp.bfloat16).astype(jnp.float32)
    bands = make_bands(weights, width).astype(jnp.bfloat16).reshape(taps * width, width)
    padded = with_halo(seafloor, (("space", 1),), half)
    windows = jnp.concatenate(
        [padded[:, shift_row : shift_row + rows_here, :] for shift_row in range(taps)], axis=2
    )
    smooth = jnp.dot(
        windows.reshape(realizations * rows_here, taps * width),
        bands,
        preferred_element_type=jnp.float32,
    )
    smooth = smooth.reshape(realizations, rows_here, width)
    return smooth * wet_mask.astype(jnp.float32)[None]


def solution(mesh):
    placed = (
        P("parts", None),
        P("parts", "space"),
        P(("parts", "space"), None, None),
        P("parts"),
        P(),
        P(("parts", "space"), None),
    )
    return jax.shard_map(
        on_device, mesh=mesh, in_specs=placed, out_specs=P("parts", "space", None), check_vma=False
    )
```

profile of v0, /device:TPU:1, one launch (start us, length us, event | category | flops | bytes accessed | tf_op | source)
XLA Modules:
  0.0 168.2 jit_solution(8644153561037456515)
XLA Ops:
  6.5 0.0 copy-start
  6.5 0.0 reduce-scatter.2.cloned.1.call-start
  6.5 13.8 %copy.24 = bf16[16,8,256,128]{3,1,2,0:T(8,128)(2,1)} copy(bf16[16,8,256,128]{3,2,1,0:T(8,128)(2,1)} %bitcast.28) | data formatting | bytes 16777216
  20.3 0.0 copy-start.2
  20.3 12.0 %copy.12 = bf16[32768,128]{1,0:T(8,128)(2,1)} copy(bf16[32768,128]{0,1:T(8,128)(2,1)} %bitcast.27) | data formatting | bytes 16777216 | tf_op jit(solution)/shard_map/dot_general | solution.py:40
  32.3 0.0 copy-done
  32.3 0.0 copy-done.2
  32.3 0.5 fusion.2
  32.9 24.5 %all_gather.3 = bf16[32,2048]{0,1:T(8,128)(2,1)S(1)} all-gather(bf16[32,128]{0,1:T(8,128)(2,1)S(1)} %fusion.2), channel_id=1, replica_groups=mesh['parts'=2,'space'=16] {'space'}, dimensions={1}, use_global_device_ids=true | all-gather | bytes 139264 | tf_op jit(solution)/shard_map/all_gather | solution.py:37
  57.3 0.8 compare_and_fusion
  58.1 0.7 gather_fusion
  58.8 0.0 copy-start.3
  58.8 8.4 %fusion.69 = f32[32,256,128]{2,0,1:T(8,128)} fusion(bf16[256,128,128]{2,1,0:T(8,128)(2,1)} %bitcast.26, bf16[128,32]{1,0:T(8,128)(2,1)S(1)} %gather_fusion, pred[128]{0:T(512)(128)(4,1)S(1)} %get-tuple-element.5), kind=kOutput, calls=%fused_computation.139 | convolution fusion | flops 268439552 | bytes 12591232 | tf_op jit(solution)/shard_map/dot_general | solution.py:40
  67.2 0.0 reduce-scatter.2.cloned.1.call-update
  67.3 0.0 copy-done.3
  67.3 0.1 copy.14
  67.4 0.6 reduce_sum.9
  68.0 0.7 fusion.74
  68.7 57.8 %gather_fusion.1 = bf16[16384,33]{1,0:T(8,128)(2,1)} fusion(bf16[33,33]{0,1:T(8,128)(2,1)S(1)} %fusion.74, s32[16384]{0:T(1024)S(1)} %fusion.62), kind=kCustom, calls=%fused_computation.1 | custom fusion | bytes 2228224 | tf_op jit(solution)/shard_map/jit(_take)/gather | solution.py:26
  126.5 0.1 fusion.67
  126.5 9.0 %reduce-scatter.2.cloned.1.call-done = f32[32,16,128]{2,0,1:T(8,128)} async-done(((f32[32,256,128]{2,0,1:T(8,128)}), f32[32,16,128]{2,0,1:T(8,128)}) %reduce-scatter.2.cloned.1.call-update) | async-done | bytes 262160 | tf_op jit(solution)/shard_map/reduce_scatter | solution.py:42
  135.5 1.0 convert_element_type.25
  136.5 4.0 %collective-permute-start = (bf16[32,16,128]{2,0,1:T(8,128)(2,1)S(1)}, bf16[32,16,128]{2,0,1:T(8,128)(2,1)S(1)}, u32[]{:S(2)}, u32[]{:S(2)}) collective-permute-start(bf16[32,16,128]{2,0,1:T(8,128)(2,1)S(1)} %convert_element_type.25), channel_id=1, source_target_pairs={{0,1},{1,2},{2,3},{3,4},{4,5},{5,6},{6,7},{7,8},{8,9},{9,10},{10,1... | collective-permute-start | bytes 393224 | tf_op jit(solution)/shard_map/ppermute | solution.py:12
  140.5 7.5 %fusion = bf16[33,128,128]{0,2,1:T(8,128)(2,1)} fusion(bf16[128,128,33]{2,1,0:T(8,128)(2,1)} %bitcast.29, pred[128,128]{1,0:T(8,128)(4,1)S(1)} %get-tuple-element.8, pred[128,128]{1,0:T(8,128)(4,1)S(1)} %get-tuple-element.7), kind=kLoop, calls=%fused_computation.4 | loop fusion | flops 1081344 | bytes 2195456 | tf_op jit(solution)/shard_map/convert_element_type | solution.py:47
  148.0 0.0 copy-start.4
  148.0 4.2 %copy.15 = bf16[33,128,128]{2,1,0:T(8,128)(2,1)S(1)} copy(bf16[33,128,128]{0,2,1:T(8,128)(2,1)} %fusion) | data formatting | bytes 2162688 | tf_op jit(solution)/shard_map/convert_element_type | solution.py:47
  152.1 0.0 copy-done.4
  152.1 0.0 copy-start.1
  152.1 2.1 %collective-permute-start.1 = (bf16[32,16,128]{2,0,1:T(8,128)(2,1)S(1)}, bf16[32,16,128]{2,0,1:T(8,128)(2,1)S(1)}, u32[]{:S(2)}, u32[]{:S(2)}) collective-permute-start(bf16[32,16,128]{2,0,1:T(8,128)(2,1)S(1)} %convert_element_type.25), channel_id=1, source_target_pairs={{1,0},{2,1},{3,2},{4,3},{5,4},{6,5},{7,6},{8,7},{9,8},{10,9},{11,1... | collective-permute-start | bytes 393224 | tf_op jit(solution)/shard_map/ppermute | solution.py:15
  154.2 0.0 collective-permute-done
  154.9 0.0 copy-done.1
  154.9 3.6 %collective-permute-done.1 = bf16[32,16,128]{2,0,1:T(8,128)(2,1)S(1)} collective-permute-done((bf16[32,16,128]{2,0,1:T(8,128)(2,1)S(1)}, bf16[32,16,128]{2,0,1:T(8,128)(2,1)S(1)}, u32[]{:S(2)}, u32[]{:S(2)}) %collective-permute-start.1) | collective-permute-done | bytes 131104 | tf_op jit(solution)/shard_map/ppermute | solution.py:15
  159.2 1.3 fusion.76
  160.5 0.9 copy_multiply_fusion
  (36 shorter events, 1.1 us)
Async XLA Ops:
  6.5 25.8 %copy-start = (bf16[4096,128]{1,0:T(8,128)(2,1)S(1)}, bf16[4096,128]{1,0:T(8,128)(2,1)}, u32[]{:S(2)}) copy-start(bf16[4096,128]{1,0:T(8,128)(2,1)} %param.7) | copy-start | bytes 3145732
  6.5 129.0 %reduce-scatter.2.cloned.1.call-start = ((), (), s32[]{:S(2)}) async-start(), calls=%async_computation.1 | async-start | bytes 4456448 | tf_op jit(solution)/shard_map/reduce_scatter | solution.py:42
  20.3 12.0 %copy-start.2 = (bf16[32,4096]{1,0:T(8,128)(2,1)S(1)}, bf16[32,4096]{1,0:T(8,128)(2,1)}, u32[]{:S(2)}) copy-start(bf16[32,4096]{1,0:T(8,128)(2,1)} %param.6) | copy-start | bytes 786436
  58.8 8.4 %copy-start.3 = (f32[33,33]{1,0:T(8,128)S(1)}, f32[33,33]{1,0:T(8,128)}, u32[]{:S(2)}) copy-start(f32[33,33]{1,0:T(8,128)} %param.10) | copy-start | bytes 13072
  136.5 17.7 %collective-permute-start = (bf16[32,16,128]{2,0,1:T(8,128)(2,1)S(1)}, bf16[32,16,128]{2,0,1:T(8,128)(2,1)S(1)}, u32[]{:S(2)}, u32[]{:S(2)}) collective-permute-start(bf16[32,16,128]{2,0,1:T(8,128)(2,1)S(1)} %convert_element_type.25), channel_id=1, source_target_pairs={{0,1},{1,2},{2,3},{3,4},{4,5},{5,6},{6,7},{7,8},{8,9},{9,10},{10,1... | collective-permute-start | bytes 393224 | tf_op jit(solution)/shard_map/ppermute | solution.py:12
  148.0 4.2 %copy-start.4 = (s32[16,128]{1,0:T(8,128)S(1)}, s32[16,128]{1,0:T(8,128)}, u32[]{:S(2)}) copy-start(s32[16,128]{1,0:T(8,128)} %param.11) | copy-start | bytes 24580
  152.1 2.7 %copy-start.1 = (f32[32,16,128]{2,0,1:T(8,128)S(1)}, f32[32,16,128]{2,0,1:T(8,128)}, u32[]{:S(2)}) copy-start(f32[32,16,128]{2,0,1:T(8,128)} %reduce-scatter.2.cloned.1.call-done) | copy-start | bytes 786436
  152.1 6.4 %collective-permute-start.1 = (bf16[32,16,128]{2,0,1:T(8,128)(2,1)S(1)}, bf16[32,16,128]{2,0,1:T(8,128)(2,1)S(1)}, u32[]{:S(2)}, u32[]{:S(2)}) collective-permute-start(bf16[32,16,128]{2,0,1:T(8,128)(2,1)S(1)} %convert_element_type.25), channel_id=1, source_target_pairs={{1,0},{2,1},{3,2},{4,3},{5,4},{6,5},{7,6},{8,7},{9,8},{10,9},{11,1... | collective-permute-start | bytes 393224 | tf_op jit(solution)/shard_map/ppermute | solution.py:15
Sparse Core Ops, SparseCore 0:
  67.4 68.0 reduce-scatter.1
where the time goes:
time: 169 us; the launch traced here: 168 us
  local copies, waits for them, and re-layouts  88.6 us (52%)
  blocking collectives  24.5 us (14%)
  between operations  13.8 us (8%)
  waiting for transfers between devices  12.6 us (7%)
  other arithmetic  12.5 us (7%)
  matrix products  10.2 us (6%)
  starting transfers between devices  6.02 us (4%)
    gather x1, local copies, waits for them, and re-layouts, make_bands(): picked = jnp.take(weights, jnp.clip(offset, 0, 2 * half), axis=1)  57.8 us
    all_gather x1, blocking collectives, on_device(): slip_all = lax.all_gather(slip, 'space', axis=1, tiled=True)  24.5 us
    unnamed x13, local copies, waits for them, and re-layouts  13.9 us
    dot_general x1, local copies, waits for them, and re-layouts, on_device(): jnp.dot(slip_rows, green.reshape(group, -1), preferred_element_type=jnp.f...  12 us
    reduce_scatter x1, waiting for transfers between devices, on_device(): lax.psum_scatter(partial_value, 'space', scatter_dimension=1, tiled=True)  8.99 us
    dot_general x1, matrix products, on_device(): jnp.dot(slip_rows, green.reshape(group, -1), preferred_element_type=jnp.f...  8.41 us
    convert_element_type x1, other arithmetic, on_device(): make_bands(weights, width).astype(jnp.bfloat16).reshape(taps * width, width)  7.48 us
    convert_element_type x1, local copies, waits for them, and re-layouts, on_device(): make_bands(weights, width).astype(jnp.bfloat16).reshape(taps * width, width)  4.15 us
  transfers between devices with their start and end apart: 3, of which 2 were waited for; matrix products, arithmetic and copies ran while one was open for 42% of the time, Pallas kernels for 0%

commit v1 on v0

v1 whole, which is shorter than its diff:
```python
import functools
import jax
import jax.numpy as jnp
from jax import lax
from jax.experimental import pallas as pl
from jax.experimental.pallas import tpu as pltpu
from jax.sharding import PartitionSpec as P

SPAN = 8


def remote(source, target, send, receive, peer):
    return pltpu.make_async_remote_copy(
        src_ref=source,
        dst_ref=target,
        send_sem=send,
        recv_sem=receive,
        device_id={"space": peer},
        device_id_type=pl.DeviceIdType.MESH,
    )


def source_kernel(
    n,
    coef_hbm, modes_hbm, green_hbm, index_ref, taps_ref, wet_ref,
    out_ref,
    coef, modes, green, slots, hots, spread, lhs, bands, rows_of,
    send_c, recv_c, keep, send_y, recv_y, send_z, recv_z, padded,
    load_sem, green_sem, slip_send, slip_recv,
    c_send, c_recv, y_send, y_recv, z_send, z_recv, halo_send, halo_recv,
):
    f32, bf16 = jnp.float32, jnp.bfloat16
    me = lax.axis_index("space")
    planes = n // 4
    z, y, c = me // 4, (me // 2) % 2, me % 2
    core_peer = me + 1 - 2 * c
    y_peer = me + 2 - 4 * y
    realizations, per = slots.shape[1], slots.shape[2]
    group, tile, width = green.shape[2], green.shape[3], green.shape[4]
    rows = tile * realizations
    taps = taps_ref.shape[0]
    half = taps // 2
    edge = half * realizations

    load_coef = pltpu.make_async_copy(coef_hbm, coef, load_sem.at[0])
    load_modes = pltpu.make_async_copy(modes_hbm, modes, load_sem.at[1])
    load_coef.start()
    load_modes.start()

    def plane_of(step):
        return lax.rem(z + 1 + step, planes)

    def green_copy(step, across, beside):
        block = plane_of(step) * 4 + ((y + beside) % 2) * 2 + (c + across) % 2
        return pltpu.make_async_copy(
            green_hbm.at[:, pl.ds(pl.multiple_of(block * tile, tile), tile), :],
            green.at[step, across * 2 + beside],
            green_sem.at[step, across * 2 + beside],
        )

    barrier = pltpu.get_barrier_semaphore()
    for k in range(1, n):
        pl.semaphore_signal(
            barrier, inc=1, device_id={"space": lax.rem(me + k, n)},
            device_id_type=pl.DeviceIdType.MESH,
        )
    for step in range(planes):
        for across in (1, 0):
            for beside in (0, 1):
                green_copy(step, across, beside).start()

    load_coef.wait()
    load_modes.wait()
    field = jnp.dot(coef[...], modes[...], preferred_element_type=f32)
    slots[me] = jnp.exp(0.5 * field).astype(bf16)
    pl.semaphore_wait(barrier, n - 1)

    def slip_copy(k):
        return remote(
            slots.at[me], slots.at[me], slip_send.at[k], slip_recv.at[k], lax.rem(me + k, n)
        )

    for k in range(1, n):
        slip_copy(k).start()

    wanted = index_ref[pl.ds(me, 1), :]
    first = lax.broadcasted_iota(jnp.int32, (per, group), 0)
    for d in range(n):
        hots[d] = (first + d * per == wanted).astype(f32).astype(bf16)
    column = lax.broadcasted_iota(jnp.int32, (group, group * tile), 1)
    owner = lax.broadcasted_iota(jnp.int32, (group, group * tile), 0)
    spread[...] = (column // tile == owner).astype(f32).astype(bf16)
    raw = taps_ref[...]
    weights = (raw / jnp.sum(raw)).astype(bf16)
    tap = lax.broadcasted_iota(jnp.int32, (taps, width), 0)
    lane = lax.broadcasted_iota(jnp.int32, (taps, width), 1)
    place = ((half - tap + width) % width == lane).astype(f32).astype(bf16)
    rows_of[...] = jnp.dot(weights, place, preferred_element_type=f32)
    source = lax.broadcasted_iota(jnp.int32, (width, width), 0)
    target = lax.broadcasted_iota(jnp.int32, (width, width), 1)
    inside = jnp.abs(source - target) <= half
    for a in range(taps):
        line = jnp.broadcast_to(rows_of[a : a + 1, :], (width, width))
        line = pltpu.roll(line, 0, 1, stride=1, stride_axis=0)
        bands[a * width : (a + 1) * width, :] = jnp.where(inside, line, 0.0).astype(bf16)

    for k in range(1, n):
        slip_copy(k).wait_recv()
    picked = jnp.zeros((realizations, group), f32)
    for d in range(n):
        picked += jnp.dot(slots[d], hots[d], preferred_element_type=f32)
    repeated = jnp.dot(picked.astype(bf16), spread[...], preferred_element_type=f32)
    inner = lax.broadcasted_iota(jnp.int32, repeated.shape, 1) % tile
    for x in range(tile):
        lhs[x * realizations : (x + 1) * realizations, :] = jnp.where(
            inner == x, repeated, 0.0
        ).astype(bf16)

    def c_copy(step):
        return remote(
            send_c.at[step], recv_c.at[step], c_send.at[step], c_recv.at[step], core_peer
        )

    def y_copy(step):
        return remote(send_y.at[step], recv_y.at[step], y_send.at[step], y_recv.at[step], y_peer)

    def z_copy(step):
        return remote(
            send_z.at[step], recv_z.at[step], z_send.at[step], z_recv.at[step],
            plane_of(step) * 4 + y * 2 + c,
        )

    def multiply(step, across):
        sides = []
        for beside in (0, 1):
            green_copy(step, across, beside).wait()
            sides.append(green[step, across * 2 + beside].reshape(group * tile, width))
        return jnp.dot(lhs[...], jnp.concatenate(sides, axis=1), preferred_element_type=f32)

    def stage(t, carry):
        @pl.when(t < planes)
        def _():
            result = multiply(t, 1)
            for beside in (0, 1):
                send_c[t, beside] = result[:, beside * width : (beside + 1) * width].astype(bf16)
            c_copy(t).start()
            result = multiply(t, 0)
            for beside in (0, 1):
                keep[t, beside] = result[:, beside * width : (beside + 1) * width]

        @pl.when((t >= 1) & (t <= planes))
        def _():
            step = t - 1
            c_copy(step).wait_recv()
            send_y[step] = (keep[step, 1] + recv_c[step, 1].astype(f32)).astype(bf16)
            y_copy(step).start()
            keep[step, 0] = keep[step, 0] + recv_c[step, 0].astype(f32)

        @pl.when((t >= 2) & (t <= planes))
        def _():
            step = t - 2
            y_copy(step).wait_recv()
            send_z[step] = (keep[step, 0] + recv_y[step].astype(f32)).astype(bf16)
            z_copy(step).start()

        return carry

    lax.fori_loop(0, planes + 1, stage, 0)
    last = planes - 1
    y_copy(last).wait_recv()
    total = keep[last, 0] + recv_y[last].astype(f32)
    for step in range(last):
        z_copy(step).wait_recv()
        total += recv_z[step].astype(f32)
    padded[edge : edge + rows, :] = total.astype(bf16)

    up = remote(
        padded.at[pl.ds(rows, edge)], padded.at[pl.ds(0, edge)],
        halo_send.at[0], halo_recv.at[0], lax.rem(me + 1, n),
    )
    down = remote(
        padded.at[pl.ds(edge, edge)], padded.at[pl.ds(edge + rows, edge)],
        halo_send.at[1], halo_recv.at[1], lax.rem(me + n - 1, n),
    )
    has_low, has_high = me > 0, me < n - 1
    pl.when(has_high)(lambda: up.start())
    pl.when(has_low)(lambda: down.start())

    @pl.when(me == 0)
    def _():
        padded[0:edge, :] = jnp.zeros((edge, width), bf16)

    @pl.when(me == n - 1)
    def _():
        padded[edge + rows :, :] = jnp.zeros((edge, width), bf16)

    pl.when(has_low)(lambda: up.wait_recv())
    pl.when(has_high)(lambda: down.wait_recv())

    smooth = None
    for begin in range(0, taps, SPAN):
        end = min(taps, begin + SPAN)
        windows = jnp.concatenate(
            [
                padded[a * realizations : a * realizations + rows, :]
                for a in range(begin, end)
            ],
            axis=1,
        )
        term = jnp.dot(
            windows, bands[begin * width : end * width, :], preferred_element_type=f32
        )
        smooth = term if smooth is None else smooth + term
    wet = wet_ref[...].astype(f32)
    for x in range(tile):
        out_ref[x] = smooth[x * realizations : (x + 1) * realizations, :] * wet[x : x + 1, :]

    for k in range(1, n):
        slip_copy(k).wait_send()
    for step in range(planes):
        c_copy(step).wait_send()
        y_copy(step).wait_send()
    for step in range(last):
        z_copy(step).wait_send()
    pl.when(has_high)(lambda: up.wait_send())
    pl.when(has_low)(lambda: down.wait_send())


def on_device(coefficients, kl_modes, green, sub_index, kernel, wet_mask):
    bf16, f32 = jnp.bfloat16, jnp.float32
    n = lax.axis_size("space")
    planes = n // 4
    realizations, modes = coefficients.shape
    per = kl_modes.shape[1]
    group, _, width = green.shape
    tile = wet_mask.shape[0]
    taps = kernel.shape[0]
    rows = tile * realizations
    edge = taps // 2 * realizations
    dma = pltpu.SemaphoreType.DMA
    vmem = pl.BlockSpec(memory_space=pltpu.VMEM)
    hbm = pl.BlockSpec(memory_space=pl.ANY)
    surface = pl.pallas_call(
        functools.partial(source_kernel, n),
        out_shape=jax.ShapeDtypeStruct((tile, realizations, width), f32),
        in_specs=[hbm, hbm, hbm, vmem, vmem, vmem],
        out_specs=vmem,
        scratch_shapes=[
            pltpu.VMEM((realizations, modes), bf16),
            pltpu.VMEM((modes, per), bf16),
            pltpu.VMEM((planes, 4, group, tile, width), bf16),
            pltpu.VMEM((n, realizations, per), bf16),
            pltpu.VMEM((n, per, group), bf16),
            pltpu.VMEM((group, group * tile), bf16),
            pltpu.VMEM((rows, group * tile), bf16),
            pltpu.VMEM((taps * width, width), bf16),
            pltpu.VMEM((taps, width), f32),
            pltpu.VMEM((planes, 2, rows, width), bf16),
            pltpu.VMEM((planes, 2, rows, width), bf16),
            pltpu.VMEM((planes, 2, rows, width), f32),
            pltpu.VMEM((planes, rows, width), bf16),
            pltpu.VMEM((planes, rows, width), bf16),
            pltpu.VMEM((planes, rows, width), bf16),
            pltpu.VMEM((planes, rows, width), bf16),
            pltpu.VMEM((rows + 2 * edge, width), bf16),
            dma((2,)),
            dma((planes, 4)),
            dma((n,)),
            dma((n,)),
            dma((planes,)),
            dma((planes,)),
            dma((planes,)),
            dma((planes,)),
            dma((planes,)),
            dma((planes,)),
            dma((2,)),
            dma((2,)),
        ],
        compiler_params=pltpu.CompilerParams(
            collective_id=0, has_side_effects=True, vmem_limit_bytes=56 * 2**20
        ),
    )(coefficients, kl_modes, green, sub_index.reshape(n, group), kernel, wet_mask)
    return surface.transpose(1, 0, 2)


def solution(mesh):
    placed = (
        P("parts", None),
        P("parts", "space"),
        P(("parts", "space"), None, None),
        P("parts"),
        P(),
        P(("parts", "space"), None),
    )
    return jax.shard_map(
        on_device, mesh=mesh, in_specs=placed, out_specs=P("parts", "space", None), check_vma=False
    )
```

time: 169 us -> 43.4 us (0.26)
  local copies, waits for them, and re-layouts: 88.6 us -> 1.81 us
  Pallas kernels: 0 us -> 41.1 us
  blocking collectives: 24.5 us -> 0 us
  between operations: 13.8 us -> 0.01 us
  waiting for transfers between devices: 12.6 us -> 0 us
  other arithmetic: 12.5 us -> 0 us
  matrix products: 10.2 us -> 0 us
  starting transfers between devices: 6.02 us -> 0 us
    gather x2 -> x0, local copies, waits for them, and re-layouts: 58.5 us -> none  [the longest x1 57.8 us: make_bands(): picked = jnp.take(weights, jnp.clip(offset, 0, 2 * half), axis=1)]
    pallas_call x0 -> x1, Pallas kernels: none -> 41.1 us  [on_device(): pl.pallas_call(functools.partial(source_kernel, n), out_shape=jax.ShapeDt...]
    all_gather x1 -> x0, blocking collectives: 24.5 us -> none  [on_device(): slip_all = lax.all_gather(slip, 'space', axis=1, tiled=True)]
    unnamed x13 -> x0, local copies, waits for them, and re-layouts: 13.9 us -> none
    dot_general x1 -> x0, local copies, waits for them, and re-layouts: 12 us -> none  [on_device(): jnp.dot(slip_rows, green.reshape(group, -1), preferred_element_type=jnp.f...]
    dot_general x3 -> x0, matrix products: 10.2 us -> none  [the longest x1 8.41 us: on_device(): jnp.dot(slip_rows, green.reshape(group, -1), preferred_element_type=jnp.f...]
    convert_element_type x4 -> x0, other arithmetic: 9.11 us -> none  [the longest x1 7.48 us: on_device(): make_bands(weights, width).astype(jnp.bfloat16).reshape(taps * width, width)]
    reduce_scatter x1 -> x0, waiting for transfers between devices: 8.99 us -> none  [on_device(): lax.psum_scatter(partial_value, 'space', scatter_dimension=1, tiled=True)]
  transfers between devices with their start and end apart: 3 -> 0, of which waited for: 2 -> 0; matrix products, arithmetic and copies ran while one was open for 42% -> 0% of each run, Pallas kernels for 0% -> 0%
where the time goes in v1:
time: 43.4 us; the launch traced here: 42.9 us
  Pallas kernels  41.1 us (95%)
  local copies, waits for them, and re-layouts  1.81 us (4%)
    pallas_call x1, Pallas kernels, on_device(): pl.pallas_call(functools.partial(source_kernel, n), out_shape=jax.ShapeDt...  41.1 us
    transpose x1, local copies, waits for them, and re-layouts, on_device(): return surface.transpose(1, 0, 2)  1.81 us

profile of v1, /device:TPU:1, one launch (start us, length us, event | category | flops | bytes accessed | tf_op | source)
XLA Modules:
  0.0 42.9 jit_solution(105374502368137651)
XLA Ops:
  0.0 41.1 %shard_map.64 = f32[16,32,128]{2,1,0:T(8,128)} custom-call(bf16[32,4096]{1,0:T(8,128)(2,1)} %coef_hbm.1, bf16[4096,128]{1,0:T(8,128)(2,1)} %modes_hbm.1, bf16[128,256,128]{2,1,0:T(8,128)(2,1)} %green_hbm.1, s32[16,128]{1,0:T(8,128)} %bitcast.3, f32[33,33]{1,0:T(8,128)} %taps_ref.1, s32[16,128]{1,0:T(8,128)} %wet_ref.1), custom_call_target="tpu_custom_call" | custom-call | tf_op jit(solution)/shard_map/pallas_call | solution.py:243
  41.1 1.8 %copy.7 = f32[32,16,128]{2,1,0:T(8,128)} copy(f32[32,16,128]{2,0,1:T(8,128)} %bitcast.2) | data formatting | bytes 524288 | tf_op jit(solution)/shard_map/transpose | solution.py:283

commit v2 on v1

--- a/solution.py
+++ b/solution.py
@@ -35,7 +35,8 @@
     z, y, c = me // 4, (me // 2) % 2, me % 2
     core_peer = me + 1 - 2 * c
     y_peer = me + 2 - 4 * y
-    realizations, per = slots.shape[1], slots.shape[2]
+    q = me % 4
+    realizations, per = slots.shape[2], slots.shape[3]
     group, tile, width = green.shape[2], green.shape[3], green.shape[4]
     rows = tile * realizations
     taps = taps_ref.shape[0]
@@ -47,8 +48,19 @@
     load_coef.start()
     load_modes.start()
 
+    middle = planes // 2
+
+    def across_planes(offset):
+        result, bit = 0, 1
+        while bit < planes:
+            result = result + ((z // bit + offset // bit) % 2) * bit
+            bit *= 2
+        return result
+
     def plane_of(step):
-        return lax.rem(z + 1 + step, planes)
+        early = jnp.where(step == middle - 1, 1, 2 * step + 3)
+        late = jnp.where(step == planes - 1, 0, 2 * (step - middle) + 2)
+        return across_planes(jnp.where(step < middle, early, late))
 
     def green_copy(step, across, beside):
         block = plane_of(step) * 4 + ((y + beside) % 2) * 2 + (c + across) % 2
@@ -72,21 +84,32 @@
     load_coef.wait()
     load_modes.wait()
     field = jnp.dot(coef[...], modes[...], preferred_element_type=f32)
-    slots[me] = jnp.exp(0.5 * field).astype(bf16)
+    slots[q, z] = jnp.exp(0.5 * field).astype(bf16)
     pl.semaphore_wait(barrier, n - 1)
 
-    def slip_copy(k):
+    def line_copy(k):
         return remote(
-            slots.at[me], slots.at[me], slip_send.at[k], slip_recv.at[k], lax.rem(me + k, n)
-        )
-
-    for k in range(1, n):
-        slip_copy(k).start()
+            slots.at[q, z], slots.at[q, z], slip_send.at[k], slip_recv.at[k],
+            lax.rem(z + k, planes) * 4 + q,
+        )
+
+    def plane_copy(k):
+        return remote(
+            slots.at[q], slots.at[q], slip_send.at[planes + k], slip_recv.at[planes + k],
+            z * 4 + lax.rem(q + k, 4),
+        )
+
+    for k in range(1, planes):
+        line_copy(k).start()
 
     wanted = index_ref[pl.ds(me, 1), :]
     first = lax.broadcasted_iota(jnp.int32, (per, group), 0)
     for d in range(n):
-        hots[d] = (first + d * per == wanted).astype(f32).astype(bf16)
+        hots[d % 4, d // 4] = (first + d * per == wanted).astype(f32).astype(bf16)
+    for k in range(1, planes):
+        line_copy(k).wait_recv()
+    for k in range(1, 4):
+        plane_copy(k).start()
     column = lax.broadcasted_iota(jnp.int32, (group, group * tile), 1)
     owner = lax.broadcasted_iota(jnp.int32, (group, group * tile), 0)
     spread[...] = (column // tile == owner).astype(f32).astype(bf16)
@@ -104,11 +127,13 @@
         line = pltpu.roll(line, 0, 1, stride=1, stride_axis=0)
         bands[a * width : (a + 1) * width, :] = jnp.where(inside, line, 0.0).astype(bf16)
 
-    for k in range(1, n):
-        slip_copy(k).wait_recv()
     picked = jnp.zeros((realizations, group), f32)
-    for d in range(n):
-        picked += jnp.dot(slots[d], hots[d], preferred_element_type=f32)
+    for k in range(4):
+        if k:
+            plane_copy(k).wait_recv()
+        held = lax.rem(q + 4 - k, 4)
+        for d in range(planes):
+            picked += jnp.dot(slots[held, d], hots[held, d], preferred_element_type=f32)
     repeated = jnp.dot(picked.astype(bf16), spread[...], preferred_element_type=f32)
     inner = lax.broadcasted_iota(jnp.int32, repeated.shape, 1) % tile
     for x in range(tile):
@@ -127,7 +152,7 @@
     def z_copy(step):
         return remote(
             send_z.at[step], recv_z.at[step], z_send.at[step], z_recv.at[step],
-            plane_of(step) * 4 + y * 2 + c,
+            jnp.where(step < middle, across_planes(1), plane_of(step)) * 4 + q,
         )
 
     def multiply(step, across):
@@ -138,38 +163,40 @@
         return jnp.dot(lhs[...], jnp.concatenate(sides, axis=1), preferred_element_type=f32)
 
     def stage(t, carry):
-        @pl.when(t < planes)
-        def _():
-            result = multiply(t, 1)
-            for beside in (0, 1):
-                send_c[t, beside] = result[:, beside * width : (beside + 1) * width].astype(bf16)
-            c_copy(t).start()
-            result = multiply(t, 0)
-            for beside in (0, 1):
-                keep[t, beside] = result[:, beside * width : (beside + 1) * width]
-
-        @pl.when((t >= 1) & (t <= planes))
+        result = multiply(t, 1)
+        for beside in (0, 1):
+            send_c[t, beside] = result[:, beside * width : (beside + 1) * width].astype(bf16)
+        c_copy(t).start()
+        result = multiply(t, 0)
+        for beside in (0, 1):
+            keep[t, beside] = result[:, beside * width : (beside + 1) * width]
+
+        c_copy(t).wait_recv()
+        send_y[t] = (keep[t, 1] + recv_c[t, 1].astype(f32)).astype(bf16)
+        y_copy(t).start()
+        keep[t, 0] = keep[t, 0] + recv_c[t, 0].astype(f32)
+
+        @pl.when(t >= 1)
         def _():
             step = t - 1
-            c_copy(step).wait_recv()
-            send_y[step] = (keep[step, 1] + recv_c[step, 1].astype(f32)).astype(bf16)
-            y_copy(step).start()
-            keep[step, 0] = keep[step, 0] + recv_c[step, 0].astype(f32)
-
-        @pl.when((t >= 2) & (t <= planes))
-        def _():
-            step = t - 2
             y_copy(step).wait_recv()
-            send_z[step] = (keep[step, 0] + recv_y[step].astype(f32)).astype(bf16)
+            keep[step, 0] = keep[step, 0] + recv_y[step].astype(f32)
+
+            @pl.when(step >= middle)
+            def _():
+                z_copy(step - middle).wait_recv()
+                keep[step, 0] = keep[step, 0] + recv_z[step - middle].astype(f32)
+
+            send_z[step] = keep[step, 0].astype(bf16)
             z_copy(step).start()
 
         return carry
 
-    lax.fori_loop(0, planes + 1, stage, 0)
+    lax.fori_loop(0, planes, stage, 0)
     last = planes - 1
     y_copy(last).wait_recv()
     total = keep[last, 0] + recv_y[last].astype(f32)
-    for step in range(last):
+    for step in range(middle - 1, last):
         z_copy(step).wait_recv()
         total += recv_z[step].astype(f32)
     padded[edge : edge + rows, :] = total.astype(bf16)
@@ -215,8 +242,10 @@
     for x in range(tile):
         out_ref[x] = smooth[x * realizations : (x + 1) * realizations, :] * wet[x : x + 1, :]
 
-    for k in range(1, n):
-        slip_copy(k).wait_send()
+    for k in range(1, planes):
+        line_copy(k).wait_send()
+    for k in range(1, 4):
+        plane_copy(k).wait_send()
     for step in range(planes):
         c_copy(step).wait_send()
         y_copy(step).wait_send()
@@ -249,8 +278,8 @@
             pltpu.VMEM((realizations, modes), bf16),
             pltpu.VMEM((modes, per), bf16),
             pltpu.VMEM((planes, 4, group, tile, width), bf16),
-            pltpu.VMEM((n, realizations, per), bf16),
-            pltpu.VMEM((n, per, group), bf16),
+            pltpu.VMEM((4, planes, realizations, per), bf16),
+            pltpu.VMEM((4, planes, per, group), bf16),
             pltpu.VMEM((group, group * tile), bf16),
             pltpu.VMEM((rows, group * tile), bf16),
             pltpu.VMEM((taps * width, width), bf16),
@@ -265,8 +294,8 @@
             pltpu.VMEM((rows + 2 * edge, width), bf16),
             dma((2,)),
             dma((planes, 4)),
-            dma((n,)),
-            dma((n,)),
+            dma((planes + 4,)),
+            dma((planes + 4,)),
             dma((planes,)),
             dma((planes,)),
             dma((planes,)),

time: 43.4 us -> 44.4 us (1.023)
  Pallas kernels: 41.1 us -> 42.4 us
    pallas_call x1, Pallas kernels: 41.1 us -> 42.4 us  [on_device(): pl.pallas_call(functools.partial(source_kernel, n), out_shape=jax.ShapeDt...]
where the time goes in v2:
time: 44.4 us; the launch traced here: 44.2 us
  Pallas kernels  42.4 us (95%)
  local copies, waits for them, and re-layouts  1.81 us (4%)
    pallas_call x1, Pallas kernels, on_device(): pl.pallas_call(functools.partial(source_kernel, n), out_shape=jax.ShapeDt...  42.4 us
    transpose x1, local copies, waits for them, and re-layouts, on_device(): return surface.transpose(1, 0, 2)  1.81 us

profile of v2, /device:TPU:1, one launch (start us, length us, event | category | flops | bytes accessed | tf_op | source)
XLA Modules:
  0.0 44.2 jit_solution(16855597674214896632)
XLA Ops:
  0.0 42.4 %shard_map.64 = f32[16,32,128]{2,1,0:T(8,128)} custom-call(bf16[32,4096]{1,0:T(8,128)(2,1)} %coef_hbm.1, bf16[4096,128]{1,0:T(8,128)(2,1)} %modes_hbm.1, bf16[128,256,128]{2,1,0:T(8,128)(2,1)} %green_hbm.1, s32[16,128]{1,0:T(8,128)} %bitcast.3, f32[33,33]{1,0:T(8,128)} %taps_ref.1, s32[16,128]{1,0:T(8,128)} %wet_ref.1), custom_call_target="tpu_custom_call" | custom-call | tf_op jit(solution)/shard_map/pallas_call | solution.py:272
  42.4 1.8 %copy.7 = f32[32,16,128]{2,1,0:T(8,128)} copy(f32[32,16,128]{2,0,1:T(8,128)} %bitcast.2) | data formatting | bytes 524288 | tf_op jit(solution)/shard_map/transpose | solution.py:312

commit v3 on v2

--- a/solution.py
+++ b/solution.py
@@ -48,19 +48,10 @@
     load_coef.start()
     load_modes.start()
 
-    middle = planes // 2
-
-    def across_planes(offset):
-        result, bit = 0, 1
-        while bit < planes:
-            result = result + ((z // bit + offset // bit) % 2) * bit
-            bit *= 2
-        return result
-
     def plane_of(step):
-        early = jnp.where(step == middle - 1, 1, 2 * step + 3)
-        late = jnp.where(step == planes - 1, 0, 2 * (step - middle) + 2)
-        return across_planes(jnp.where(step < middle, early, late))
+        middle = planes // 2
+        ahead = jnp.where(step == 0, middle, jnp.where(step < middle, step, step + 1))
+        return lax.rem(z + ahead, planes)
 
     def green_copy(step, across, beside):
         block = plane_of(step) * 4 + ((y + beside) % 2) * 2 + (c + across) % 2
@@ -152,7 +143,7 @@
     def z_copy(step):
         return remote(
             send_z.at[step], recv_z.at[step], z_send.at[step], z_recv.at[step],
-            jnp.where(step < middle, across_planes(1), plane_of(step)) * 4 + q,
+            plane_of(step) * 4 + y * 2 + c,
         )
 
     def multiply(step, across):
@@ -180,14 +171,7 @@
         def _():
             step = t - 1
             y_copy(step).wait_recv()
-            keep[step, 0] = keep[step, 0] + recv_y[step].astype(f32)
-
-            @pl.when(step >= middle)
-            def _():
-                z_copy(step - middle).wait_recv()
-                keep[step, 0] = keep[step, 0] + recv_z[step - middle].astype(f32)
-
-            send_z[step] = keep[step, 0].astype(bf16)
+            send_z[step] = (keep[step, 0] + recv_y[step].astype(f32)).astype(bf16)
             z_copy(step).start()
 
         return carry
@@ -196,7 +180,7 @@
     last = planes - 1
     y_copy(last).wait_recv()
     total = keep[last, 0] + recv_y[last].astype(f32)
-    for step in range(middle - 1, last):
+    for step in range(last):
         z_copy(step).wait_recv()
         total += recv_z[step].astype(f32)
     padded[edge : edge + rows, :] = total.astype(bf16)

time: 44.4 us -> 41.9 us (0.944)
  Pallas kernels: 42.4 us -> 39.8 us
    pallas_call x1, Pallas kernels: 42.4 us -> 39.8 us  [on_device(): pl.pallas_call(functools.partial(source_kernel, n), out_shape=jax.ShapeDt...]
where the time goes in v3:
time: 41.9 us; the launch traced here: 41.7 us
  Pallas kernels  39.8 us (95%)
  local copies, waits for them, and re-layouts  1.81 us (4%)
    pallas_call x1, Pallas kernels, on_device(): pl.pallas_call(functools.partial(source_kernel, n), out_shape=jax.ShapeDt...  39.8 us
    transpose x1, local copies, waits for them, and re-layouts, on_device(): return surface.transpose(1, 0, 2)  1.81 us

profile of v3, /device:TPU:1, one launch (start us, length us, event | category | flops | bytes accessed | tf_op | source)
XLA Modules:
  0.0 41.7 jit_solution(16020013082889175458)
XLA Ops:
  0.0 39.8 %shard_map.64 = f32[16,32,128]{2,1,0:T(8,128)} custom-call(bf16[32,4096]{1,0:T(8,128)(2,1)} %coef_hbm.1, bf16[4096,128]{1,0:T(8,128)(2,1)} %modes_hbm.1, bf16[128,256,128]{2,1,0:T(8,128)(2,1)} %green_hbm.1, s32[16,128]{1,0:T(8,128)} %bitcast.3, f32[33,33]{1,0:T(8,128)} %taps_ref.1, s32[16,128]{1,0:T(8,128)} %wet_ref.1), custom_call_target="tpu_custom_call" | custom-call | tf_op jit(solution)/shard_map/pallas_call | solution.py:256
  39.9 1.8 %copy.7 = f32[32,16,128]{2,1,0:T(8,128)} copy(f32[32,16,128]{2,0,1:T(8,128)} %bitcast.2) | data formatting | bytes 524288 | tf_op jit(solution)/shard_map/transpose | solution.py:296

commit v4 on v3

--- a/solution.py
+++ b/solution.py
@@ -162,17 +162,17 @@
         for beside in (0, 1):
             keep[t, beside] = result[:, beside * width : (beside + 1) * width]
 
-        c_copy(t).wait_recv()
-        send_y[t] = (keep[t, 1] + recv_c[t, 1].astype(f32)).astype(bf16)
-        y_copy(t).start()
-        keep[t, 0] = keep[t, 0] + recv_c[t, 0].astype(f32)
-
         @pl.when(t >= 1)
         def _():
             step = t - 1
             y_copy(step).wait_recv()
             send_z[step] = (keep[step, 0] + recv_y[step].astype(f32)).astype(bf16)
             z_copy(step).start()
+
+        c_copy(t).wait_recv()
+        send_y[t] = (keep[t, 1] + recv_c[t, 1].astype(f32)).astype(bf16)
+        y_copy(t).start()
+        keep[t, 0] = keep[t, 0] + recv_c[t, 0].astype(f32)
 
         return carry
 

time: 41.9 us -> 41.9 us (level)
  no operation moved by 1% of the time
where the time goes in v4:
time: 41.9 us; the launch traced here: 41.7 us
  Pallas kernels  39.8 us (95%)
  local copies, waits for them, and re-layouts  1.81 us (4%)
    pallas_call x1, Pallas kernels, on_device(): pl.pallas_call(functools.partial(source_kernel, n), out_shape=jax.ShapeDt...  39.8 us
    transpose x1, local copies, waits for them, and re-layouts, on_device(): return surface.transpose(1, 0, 2)  1.81 us

profile of v4, /device:TPU:1, one launch (start us, length us, event | category | flops | bytes accessed | tf_op | source)
XLA Modules:
  0.0 41.7 jit_solution(11635363956934643672)
XLA Ops:
  0.0 39.8 %shard_map.64 = f32[16,32,128]{2,1,0:T(8,128)} custom-call(bf16[32,4096]{1,0:T(8,128)(2,1)} %coef_hbm.1, bf16[4096,128]{1,0:T(8,128)(2,1)} %modes_hbm.1, bf16[128,256,128]{2,1,0:T(8,128)(2,1)} %green_hbm.1, s32[16,128]{1,0:T(8,128)} %bitcast.3, f32[33,33]{1,0:T(8,128)} %taps_ref.1, s32[16,128]{1,0:T(8,128)} %wet_ref.1), custom_call_target="tpu_custom_call" | custom-call | tf_op jit(solution)/shard_map/pallas_call | solution.py:256
  39.9 1.8 %copy.7 = f32[32,16,128]{2,1,0:T(8,128)} copy(f32[32,16,128]{2,0,1:T(8,128)} %bitcast.2) | data formatting | bytes 524288 | tf_op jit(solution)/shard_map/transpose | solution.py:296
